TPU v7x, 128 devices: a whole 4x4x4 slice. The times are simulated.
128 devices in a mesh: row: 16 (over y, x), col: 8 (over z, core).
Axes of the slice: x: 4, y: 4, z: 4, core: 2. Of those that a mesh axis runs over, the one named last changes fastest.
Arguments:
- layer_input: bfloat16 [768, 8192], P('col', 'row'), may hold values from -6 to 6
- out_grad: bfloat16 [768, 8192], P('col', 'row'), may hold values from -4 to 4
- head_depth: int32 [768], P('col'), may hold values from 0 to 4
- gate_weight: bfloat16 [8192, 28672], P('row', 'col'), may hold values from -0.0625 to 0.0625
- up_weight: bfloat16 [8192, 28672], P('row', 'col'), may hold values from -0.0625 to 0.0625
- down_weight: bfloat16 [28672, 8192], P('col', 'row'), may hold values from -0.03125 to 0.03125
Outputs:
- grad_input: bfloat16 [768, 8192], P('col', 'row')
- grad_gate: bfloat16 [8192, 28672], P('row', 'col')
- grad_up: bfloat16 [8192, 28672], P('row', 'col')
- grad_down: bfloat16 [28672, 8192], P('col', 'row')
All inputs are finite; a program needn't handle non-finite values.
Results may differ from a plain program's by a relative error of at most 0.033.
Values may be sent and summed in bfloat16 or wider, within the bound.
A program may use at most 128 MiB of HBM per device.

v0:
```python
import jax
import jax.numpy as jnp
from jax import lax
from jax.sharding import PartitionSpec as P


def activate(gate_sum, up_sum, back_sum):
    sigmoid_val = jax.nn.sigmoid(gate_sum)
    silu_val = gate_sum * sigmoid_val
    hidden = (silu_val * up_sum).astype(jnp.bfloat16)
    slope = sigmoid_val * (1.0 + gate_sum * (1.0 - sigmoid_val))
    gate_act = (back_sum * up_sum * slope).astype(jnp.bfloat16)
    up_act = (back_sum * silu_val).astype(jnp.bfloat16)
    return (hidden, gate_act, up_act)


def body(layer_input, out_grad, head_depth, gate_weight, up_weight, down_weight):
    contract_rows = (((0,), (0,)), ((), ()))
    contract_cols = (((1,), (1,)), ((), ()))
    weighting = jnp.power(jnp.float32(0.8), head_depth.astype(jnp.float32))
    scaled = (out_grad.astype(jnp.float32) * weighting[:, None]).astype(jnp.bfloat16)
    inputs_all, grads_all = (
        lax.all_gather(layer_input, "col", axis=0, tiled=True),
        lax.all_gather(scaled, "col", axis=0, tiled=True),
    )
    gate_part = jnp.dot(inputs_all, gate_weight, preferred_element_type=jnp.float32)
    up_part = jnp.dot(inputs_all, up_weight, preferred_element_type=jnp.float32)
    back_part = lax.dot_general(
        grads_all, down_weight, contract_cols, preferred_element_type=jnp.float32
    )
    gate_sum, up_sum, back_sum = (
        lax.psum(gate_part.astype(jnp.bfloat16), "row").astype(jnp.float32),
        lax.psum(up_part.astype(jnp.bfloat16), "row").astype(jnp.float32),
        lax.psum(back_part.astype(jnp.bfloat16), "row").astype(jnp.float32),
    )
    hidden, gate_act, up_act = activate(gate_sum, up_sum, back_sum)
    grad_down = lax.dot_general(
        hidden, grads_all, contract_rows, preferred_element_type=jnp.float32
    ).astype(jnp.bfloat16)
    grad_gate = lax.dot_general(
        inputs_all, gate_act, contract_rows, preferred_element_type=jnp.float32
    ).astype(jnp.bfloat16)
    grad_up = lax.dot_general(
        inputs_all, up_act, contract_rows, preferred_element_type=jnp.float32
    ).astype(jnp.bfloat16)
    input_part = lax.dot_general(
        gate_act, gate_weight, contract_cols, preferred_element_type=jnp.float32
    )
    input_part = input_part + lax.dot_general(
        up_act, up_weight, contract_cols, preferred_element_type=jnp.float32
    )
    grad_input = lax.psum_scatter(
        input_part.astype(jnp.bfloat16), "col", scatter_dimension=0, tiled=True
    )
    return (grad_input, grad_gate, grad_up, grad_down)


def solution(mesh):
    in_specs = (
        P("col", "row"),
        P("col", "row"),
        P("col"),
        P("row", "col"),
        P("row", "col"),
        P("col", "row"),
    )
    out_specs = (P("col", "row"), P("row", "col"), P("row", "col"), P("col", "row"))
    return jax.shard_map(body, mesh=mesh, in_specs=in_specs, out_specs=out_specs, check_vma=False)
```

profile of v0, /device:TPU:0, one launch (start us, length us, event | category | flops | bytes accessed | tf_op | source)
XLA Modules:
  0.0 349.1 jit_solution(12524002393062290515)
XLA Ops:
  7.2 0.0 all-reduce.3.cloned.1.call-start
  7.2 0.7 convert_power_fusion
  7.9 1.0 multiply_convert_fusion
  8.9 14.7 %all_gather.6 = bf16[768,512]{1,0:T(8,128)(2,1)S(1)} all-gather(bf16[96,512]{1,0:T(8,128)(2,1)S(1)} %multiply_convert_fusion), channel_id=1, replica_groups=mesh['row'=16,'col'=8] {'col'}, dimensions={0}, use_global_device_ids=true | all-gather | bytes 884736 | tf_op jit(solution)/shard_map/all_gather | solution.py:24
  23.5 13.6 %all_gather.7 = bf16[768,512]{1,0:T(8,128)(2,1)S(1)} all-gather(bf16[96,512]{1,0:T(8,128)(2,1)} %param.6), channel_id=1, replica_groups=mesh['row'=16,'col'=8] {'col'}, dimensions={0}, use_global_device_ids=true | all-gather | bytes 884736 | tf_op jit(solution)/shard_map/all_gather | solution.py:23
  37.1 6.9 %convolution_convert_fusion = bf16[768,3584]{1,0:T(8,128)(2,1)} fusion(bf16[768,512]{1,0:T(8,128)(2,1)S(1)} %all_gather.7, bf16[512,3584]{1,0:T(8,128)(2,1)} %param.9), kind=kOutput, calls=%fused_computation.15 | convolution fusion | flops 2821324800 | bytes 9961472 | tf_op jit(solution)/shard_map/dot_general | solution.py:26
  44.0 0.0 copy-done.2
  44.0 4.8 %convolution_convert_fusion.1 = bf16[768,3584]{1,0:T(8,128)(2,1)} fusion(bf16[768,512]{1,0:T(8,128)(2,1)S(1)} %all_gather.7, bf16[512,3584]{1,0:T(8,128)(2,1)S(1)} %copy-done.2), kind=kOutput, calls=%fused_computation.16 | convolution fusion | flops 2821324800 | bytes 9961472 | tf_op jit(solution)/shard_map/dot_general | solution.py:27
  48.8 0.0 copy-done
  48.8 4.9 %convolution_convert_fusion.2 = bf16[768,3584]{1,0:T(8,128)(2,1)} fusion(bf16[768,512]{1,0:T(8,128)(2,1)S(1)} %all_gather.6, bf16[3584,512]{1,0:T(8,128)(2,1)S(1)} %copy-done), kind=kOutput, calls=%fused_computation.17 | convolution fusion | flops 2821324800 | bytes 9961472 | tf_op jit(solution)/shard_map/dot_general | solution.py:28
  53.7 0.0 all-reduce.3.cloned.1.call-update
  53.7 0.2 reduce-scatter.2.cloned.1.call-start
  54.0 219.5 %all-reduce.3.cloned.1.call-done = (bf16[768,3584]{1,0:T(8,128)(2,1)}, bf16[768,3584]{1,0:T(8,128)(2,1)}, bf16[768,3584]{1,0:T(8,128)(2,1)}) async-done(((bf16[768,3584]{1,0:T(8,128)(2,1)}, bf16[768,3584]{1,0:T(8,128)(2,1)}, bf16[768,3584]{1,0:T(8,128)(2,1)}), (bf16[768,3584]{1,0:T(8,128)(2,1)}, bf16[768,3584]{1,0:T(8,128)(2,1)}, bf16[768,3584]{1,0:T(8,128)(2,1)})) %all-reduce.3.cloned.1.call-update) | async-done | bytes 16515088 | tf_op jit(solution)/shard_map/psum | solution.py:33
  273.5 9.3 %fusion = (bf16[768,3584]{1,0:T(8,128)(2,1)S(1)}, bf16[768,3584]{1,0:T(8,128)(2,1)S(1)}) fusion(bf16[768,3584]{1,0:T(8,128)(2,1)} %get-tuple-element.9, bf16[768,3584]{1,0:T(8,128)(2,1)} %get-tuple-element.10, bf16[768,3584]{1,0:T(8,128)(2,1)} %get-tuple-element.8), kind=kLoop, calls=%fused_computation.6 | loop fusion | flops 44040192 | bytes 27525120 | tf_op jit(solution)/shard_map/convert_element_type | solution.py:13
  282.8 0.0 copy-done.1
  282.8 3.0 fusion.13
  285.8 4.6 %fusion.10 = bf16[512,3584]{0,1:T(8,128)(2,1)} fusion(bf16[768,3584]{1,0:T(8,128)(2,1)S(1)} %get-tuple-element.12, bf16[768,512]{1,0:T(8,128)(2,1)S(1)} %all_gather.7), kind=kOutput, calls=%fused_computation.21 | convolution fusion | flops 2820407296 | bytes 9961472 | tf_op jit(solution)/shard_map/dot_general | solution.py:40
  290.4 4.5 %fusion.11 = bf16[512,3584]{0,1:T(8,128)(2,1)} fusion(bf16[768,3584]{1,0:T(8,128)(2,1)S(1)} %get-tuple-element.11, bf16[768,512]{1,0:T(8,128)(2,1)S(1)} %all_gather.7), kind=kOutput, calls=%fused_computation.22 | convolution fusion | flops 2820407296 | bytes 9961472 | tf_op jit(solution)/shard_map/dot_general | solution.py:43
  294.9 3.9 %add_convert_fusion = bf16[768,512]{1,0:T(8,128)(2,1)} fusion(f32[768,512]{1,0:T(8,128)S(1)} %fusion.13, bf16[768,3584]{1,0:T(8,128)(2,1)S(1)} %get-tuple-element.11, bf16[512,3584]{1,0:T(8,128)(2,1)S(1)} %copy-done.3), kind=kOutput, calls=%fused_computation.23 | convolution fusion | flops 2819358720 | bytes 11534336 | tf_op jit(solution)/shard_map/dot_general | solution.py:49
  298.8 5.9 %copy.11 = bf16[512,3584]{1,0:T(8,128)(2,1)} copy(bf16[512,3584]{0,1:T(8,128)(2,1)} %fusion.11) | data formatting | bytes 7340032
  304.8 5.9 %copy.10 = bf16[512,3584]{1,0:T(8,128)(2,1)} copy(bf16[512,3584]{0,1:T(8,128)(2,1)} %fusion.10) | data formatting | bytes 7340032
  310.7 0.0 reduce-scatter.2.cloned.1.call-update
  310.7 10.9 %convolution_convert_fusion.3 = bf16[3584,512]{1,0:T(8,128)(2,1)} fusion(bf16[768,512]{1,0:T(8,128)(2,1)S(1)} %all_gather.6, bf16[768,3584]{1,0:T(8,128)(2,1)} %get-tuple-element.8, bf16[768,3584]{1,0:T(8,128)(2,1)} %get-tuple-element.10), kind=kOutput, calls=%fused_computation.18 | convolution fusion | flops 2842427392 | bytes 15466496 | tf_op jit(solution)/shard_map/dot_general | solution.py:37
  321.6 20.6 %reduce-scatter.2.cloned.1.call-done = bf16[96,512]{1,0:T(8,128)(2,1)} async-done(((bf16[768,512]{1,0:T(8,128)(2,1)}), bf16[96,512]{1,0:T(8,128)(2,1)}) %reduce-scatter.2.cloned.1.call-update) | async-done | bytes 98320 | tf_op jit(solution)/shard_map/reduce_scatter | solution.py:52
  (5 shorter events, 0.0 us)
Async XLA Ops:
  7.2 266.3 %all-reduce.3.cloned.1.call-start = ((), (), s32[]{:S(2)}) async-start(), calls=%async_computation.2 | async-start | bytes 33030144 | tf_op jit(solution)/shard_map/psum | solution.py:33
  37.1 6.9 %copy-start.2 = (bf16[512,3584]{1,0:T(8,128)(2,1)S(1)}, bf16[512,3584]{1,0:T(8,128)(2,1)}, u32[]{:S(2)}) copy-start(bf16[512,3584]{1,0:T(8,128)(2,1)} %param.10) | copy-start | bytes 11010052
  44.0 4.8 %copy-start = (bf16[3584,512]{1,0:T(8,128)(2,1)S(1)}, bf16[3584,512]{1,0:T(8,128)(2,1)}, u32[]{:S(2)}) copy-start(bf16[3584,512]{1,0:T(8,128)(2,1)} %param.11) | copy-start | bytes 11010052
  53.7 288.5 %reduce-scatter.2.cloned.1.call-start = ((), (), s32[]{:S(2)}) async-start(), calls=%async_computation.1 | async-start | bytes 884736 | tf_op jit(solution)/shard_map/reduce_scatter | solution.py:52
  273.5 9.3 %copy-start.1 = (bf16[512,3584]{1,0:T(8,128)(2,1)S(1)}, bf16[512,3584]{1,0:T(8,128)(2,1)}, u32[]{:S(2)}) copy-start(bf16[512,3584]{1,0:T(8,128)(2,1)} %param.9) | copy-start | bytes 11010052
  290.4 4.5 %copy-start.3 = (bf16[512,3584]{1,0:T(8,128)(2,1)S(1)}, bf16[512,3584]{1,0:T(8,128)(2,1)}, u32[]{:S(2)}) copy-start(bf16[512,3584]{1,0:T(8,128)(2,1)} %param.10) | copy-start | bytes 11010052
Sparse Core Ops, SparseCore 0:
  53.9 219.5 all-reduce.2
  310.8 31.3 reduce-scatter.1
where the time goes:
time: 349 us
  waiting for transfers between devices  240 us (69%)
  matrix products  43.5 us (12%)
  blocking collectives  28.3 us (8%)
  between operations  14.1 us (4%)
  local copies, waits for them, and re-layouts  11.8 us (3%)
  other arithmetic  10.9 us (3%)
    psum x1, waiting for transfers between devices, body(): lax.psum(up_part.astype(jnp.bfloat16), 'row').astype(jnp.float32)  219 us
    reduce_scatter x1, waiting for transfers between devices, body(): lax.psum_scatter(input_part.astype(jnp.bfloat16), 'col', scatter_dimensio...  20.6 us
    all_gather x1, blocking collectives, body(): lax.all_gather(scaled, 'col', axis=0, tiled=True)  14.7 us
    all_gather x1, blocking collectives, body(): lax.all_gather(layer_input, 'col', axis=0, tiled=True)  13.6 us
    unnamed x10, local copies, waits for them, and re-layouts  11.8 us
    dot_general x1, matrix products, body(): lax.dot_general(hidden, grads_all, contract_rows, preferred_element_type=...  10.9 us
    convert_element_type x1, other arithmetic, activate(): up_act = (back_sum * silu_val).astype(jnp.bfloat16)  9.29 us
  transfers between devices with their start and end apart: 2, of which 2 were waited for; matrix products, arithmetic and copies ran while one was open for 3% of the time, Pallas kernels for 0%

commit v1 on v0

v1 whole, which is shorter than its diff:
```python
import functools

import jax
import jax.numpy as jnp
from jax import lax
from jax.experimental import pallas as pl
from jax.experimental.pallas import tpu as pltpu
from jax.sharding import PartitionSpec as P

MESH = pl.DeviceIdType.MESH
BF = jnp.bfloat16
F32 = jnp.float32

T = 768
DB = 512
FB = 3584
TB = 96
PART = FB // 4
GROUPS = ((0, 384), (384, 256), (640, 256))
NG = len(GROUPS)
ROFF = (0, 384, 576, 672)

ORDER = (
    ("fwd", 0), ("fwd", 1),
    ("rs", 0, 0), ("fwd", 2), ("rs", 1, 0), ("rs", 0, 1), ("rs", 2, 0), ("rs", 1, 1), ("rs", 0, 2),
    ("rs", 0, 3), ("rs", 2, 1), ("rs", 1, 2), ("ag", 0, 3), ("rs", 1, 3), ("rs", 2, 2),
    ("ag", 0, 2), ("rs", 2, 3), ("ag", 1, 3), ("ag", 0, 1), ("ag", 2, 3), ("ag", 1, 2), ("ag", 2, 2),
    ("ag", 1, 1), ("ag", 0, 0), ("grad", 0), ("ag", 2, 1), ("ag", 1, 0), ("grad", 1), ("ag", 2, 0), ("grad", 2),
)


def nt(a, b):
    return lax.dot_general(a, b, (((1,), (1,)), ((), ())), preferred_element_type=F32)


def nn(a, b):
    return jnp.dot(a, b, preferred_element_type=F32)


def kernel(
    x_ref, og_ref, hd_ref, wg_hbm, wu_hbm, wd_hbm,
    gi_ref, dg_hbm, du_hbm, dd_hbm,
    S, R, XS, XT, WG, WU, WD, GI, GB, GR,
    wsem, zs, zr, cs, cr, ss, sr, gs, gr, osem, free,
):
    row = lax.axis_index("row")
    col = lax.axis_index("col")
    x = lax.rem(row, 4)
    y = row // 4
    z = col // 2
    c = lax.rem(col, 2)
    rows_of = (
        y * 4 + x + 1 - 2 * lax.rem(x, 2),
        (y + 1 - 2 * lax.rem(y, 2)) * 4 + x,
        y * 4 + 3 - x,
        (3 - y) * 4 + x,
    )
    bits = (lax.rem((x + 1) // 2, 2), lax.rem((y + 1) // 2, 2), x // 2, y // 2)

    def pick(values, d):
        return jnp.where(d == 0, values[0], jnp.where(d == 1, values[1], jnp.where(d == 2, values[2], values[3])))

    def low(p, k):
        at = jnp.int32(0)
        for i in range(k):
            at = at + pick(bits, lax.rem(p + i, 4)) * (T >> (i + 1))
        return at

    def columns(j, p):
        return pl.ds(pl.multiple_of(p * PART + GROUPS[j][0], 128), GROUPS[j][1])

    def rows(at, n):
        return pl.ds(pl.multiple_of(at, 48), n)

    def rs_copy(j, k, p):
        n = T >> (k + 1)
        at = low(p, k) + (1 - pick(bits, lax.rem(p + k, 4))) * n
        return pltpu.make_async_remote_copy(
            src_ref=S.at[:, rows(at, n), columns(j, p)],
            dst_ref=R.at[:, pl.ds(ROFF[k], n), columns(j, p)],
            send_sem=ss.at[j, k, p], recv_sem=sr.at[j, k, p],
            device_id=(pick(rows_of, lax.rem(p + k, 4)), col), device_id_type=MESH,
        )

    def ag_copy(j, k, p):
        n = T >> (k + 1)
        where = S.at[:, rows(low(p, k + 1), n), columns(j, p)]
        return pltpu.make_async_remote_copy(
            src_ref=where, dst_ref=where,
            send_sem=ss.at[j, 7 - k, p], recv_sem=sr.at[j, 7 - k, p],
            device_id=(pick(rows_of, lax.rem(p + k, 4)), col), device_id_type=MESH,
        )

    loads = [
        pltpu.make_async_copy(src, dst, wsem.at[i])
        for i, (src, dst) in enumerate(((wg_hbm, WG), (wu_hbm, WU), (wd_hbm, WD)))
    ]
    for load in loads:
        load.start()

    barrier = pltpu.get_barrier_semaphore()
    for r in rows_of:
        pl.semaphore_signal(barrier, inc=1, device_id=(r, col), device_id_type=MESH)
    others = []
    for dz in range(4):
        for dc in range(2):
            if dz + dc > 0:
                others.append((row, lax.rem(z + dz, 4) * 2 + lax.rem(c + dc, 2)))
    for device in others:
        pl.semaphore_signal(barrier, inc=1, device_id=device, device_id_type=MESH)

    depth = jnp.broadcast_to(hd_ref[...], (128, TB))
    weight = jnp.ones((128, TB), F32)
    for level in range(1, 5):
        weight = jnp.where(depth == level, F32(0.8) ** level, weight)
    weight = weight.T
    mine = pl.ds(pl.multiple_of(col * TB, TB), TB)
    XS[0, mine, :] = x_ref[...]
    for i in range(DB // 128):
        at = slice(i * 128, (i + 1) * 128)
        XS[1, mine, at] = (og_ref[:, at].astype(F32) * weight).astype(BF)

    pl.semaphore_wait(barrier, 11)

    def z_copy(dz):
        return pltpu.make_async_remote_copy(
            src_ref=XS.at[:, mine], dst_ref=XS.at[:, mine],
            send_sem=zs.at[dz], recv_sem=zr.at[dz],
            device_id=(row, lax.rem(z + dz, 4) * 2 + c), device_id_type=MESH,
        )

    def c_copy(dz):
        where = XS.at[:, pl.ds(pl.multiple_of((lax.rem(z + 4 - dz, 4) * 2 + c) * TB, TB), TB)]
        return pltpu.make_async_remote_copy(
            src_ref=where, dst_ref=where, send_sem=cs.at[dz], recv_sem=cr.at[dz],
            device_id=(row, z * 2 + 1 - c), device_id_type=MESH,
        )

    for dz in (1, 3, 2):
        z_copy(dz).start()
    c_copy(0).start()
    for dz in (1, 3, 2):
        z_copy(dz).wait_recv()
        c_copy(dz).start()
    for load in loads:
        load.wait()
    for dz in range(4):
        c_copy(dz).wait_recv()

    GI[...] = jnp.zeros_like(GI)

    def forward(j, p, at):
        r = rows(at, T // 2)
        cols = columns(j, p)
        S[0, r, cols] = nn(XS[0, r, :], WG[:, cols]).astype(BF)
        S[1, r, cols] = nn(XS[0, r, :], WU[:, cols]).astype(BF)
        S[2, r, cols] = nt(XS[1, r, :], WD[cols, :]).astype(BF)

    def fwd(j):
        @pl.loop(0, 4)
        def _(p):
            forward(j, p, (1 - pick(bits, p)) * (T // 2))
            rs_copy(j, 0, p).start()

        @pl.loop(0, 4)
        def _(p):
            forward(j, p, pick(bits, p) * (T // 2))

    def rs(j, k):
        n = T >> (k + 1)

        @pl.loop(0, 4)
        def _(p):
            rs_copy(j, k, p).wait_recv()
            cols = columns(j, p)
            at = low(p, k + 1)
            if k < 3:
                @pl.loop(0, n // 48)
                def _(i):
                    r = rows(at + i * 48, 48)
                    q = rows(ROFF[k] + i * 48, 48)
                    S[:, r, cols] = (S[:, r, cols].astype(F32) + R[:, q, cols].astype(F32)).astype(BF)

                rs_copy(j, k + 1, p).start()
            else:
                r = rows(at, 48)
                q = pl.ds(ROFF[3], 48)
                gate = S[0, r, cols].astype(F32) + R[0, q, cols].astype(F32)
                up = S[1, r, cols].astype(F32) + R[1, q, cols].astype(F32)
                back = S[2, r, cols].astype(F32) + R[2, q, cols].astype(F32)
                sig = jax.nn.sigmoid(gate)
                silu = gate * sig
                S[0, r, cols] = (silu * up).astype(BF)
                S[1, r, cols] = (back * up * (sig * (1.0 + gate * (1.0 - sig)))).astype(BF)
                S[2, r, cols] = (back * silu).astype(BF)
            rs_copy(j, k, p).wait_send()
            pl.semaphore_signal(
                free.at[j, k, p], inc=1,
                device_id=(pick(rows_of, lax.rem(p + k, 4)), col), device_id_type=MESH,
            )
        if k == 3:
            @pl.loop(0, 4)
            def _(p):
                gather(j, 3, p)

    def gather(j, k, p):
        pl.semaphore_wait(free.at[j, k, p], 1)
        ag_copy(j, k, p).start()

    def ag(j, k):
        @pl.loop(0, 4)
        def _(p):
            ag_copy(j, k, p).wait_recv()
            if k > 0:
                gather(j, k - 1, p)

    def out_copies(j, p):
        cols = columns(j, p)
        return (
            pltpu.make_async_copy(WG.at[:, cols], dg_hbm.at[:, cols], osem.at[j, 0, p]),
            pltpu.make_async_copy(WU.at[:, cols], du_hbm.at[:, cols], osem.at[j, 1, p]),
            pltpu.make_async_copy(WD.at[cols, :], dd_hbm.at[cols, :], osem.at[j, 2, p]),
        )

    def input_grad(j):
        @pl.loop(0, 4)
        def _(p):
            cols = columns(j, p)

            @pl.loop(0, 3)
            def _(i):
                r = pl.ds(pl.multiple_of(i * 256, 256), 256)
                GI[r, :] = GI[r, :] + nt(S[1, r, cols], WG[:, cols]) + nt(S[2, r, cols], WU[:, cols])

    def weight_grads(j):
        @pl.loop(0, 4)
        def _(p):
            cols = columns(j, p)
            WG[:, cols] = nn(XT[0], S[1, :, cols]).astype(BF)
            WU[:, cols] = nn(XT[0], S[2, :, cols]).astype(BF)
            WD[cols, :] = nn(XT[1], S[0, :, cols]).astype(BF).T
            for copy in out_copies(j, p):
                copy.start()

    def gi_copy(i):
        device = others[i]
        return pltpu.make_async_remote_copy(
            src_ref=GB.at[pl.ds(pl.multiple_of(device[1] * TB, TB), TB)], dst_ref=GR.at[i],
            send_sem=gs.at[i], recv_sem=gr.at[i], device_id=device, device_id_type=MESH,
        )

    for step in ORDER:
        what, j = step[:2]
        if what == "fwd":
            fwd(j)
            if j == NG - 1:
                XT[0] = XS[0].T
                XT[1] = XS[1].T
        elif what == "rs":
            rs(j, step[2])
        elif what == "ag":
            ag(j, step[2])
        else:
            input_grad(j)
            if j == NG - 1:
                GB[...] = GI[...].astype(BF)
                for i in range(7):
                    gi_copy(i).start()
            weight_grads(j)

    total = GI[mine, :]
    for i in range(7):
        gi_copy(i).wait_recv()
        total = total + GR[i].astype(F32)
    gi_ref[...] = total.astype(BF)

    for j in range(NG):
        @pl.loop(0, 4)
        def _(p):
            for copy in out_copies(j, p):
                copy.wait()
            for k in range(4):
                ag_copy(j, k, p).wait_send()
    for i in range(7):
        gi_copy(i).wait_send()
    for dz in range(4):
        if dz > 0:
            z_copy(dz).wait_send()
        c_copy(dz).wait_send()


def body(layer_input, out_grad, head_depth, gate_weight, up_weight, down_weight):
    vmem = pl.BlockSpec(memory_space=pltpu.VMEM)
    hbm = pl.BlockSpec(memory_space=pl.ANY)
    dma = pltpu.SemaphoreType.DMA
    return pl.pallas_call(
        kernel,
        out_shape=(
            jax.ShapeDtypeStruct((TB, DB), BF),
            jax.ShapeDtypeStruct((DB, FB), BF),
            jax.ShapeDtypeStruct((DB, FB), BF),
            jax.ShapeDtypeStruct((FB, DB), BF),
        ),
        in_specs=[vmem, vmem, vmem, hbm, hbm, hbm],
        out_specs=(vmem, hbm, hbm, hbm),
        scratch_shapes=[
            pltpu.VMEM((3, T, FB), BF),
            pltpu.VMEM((3, 720, FB), BF),
            pltpu.VMEM((2, T, DB), BF),
            pltpu.VMEM((2, DB, T), BF),
            pltpu.VMEM((DB, FB), BF),
            pltpu.VMEM((DB, FB), BF),
            pltpu.VMEM((FB, DB), BF),
            pltpu.VMEM((T, DB), F32),
            pltpu.VMEM((T, DB), BF),
            pltpu.VMEM((7, TB, DB), BF),
            dma((3,)), dma((4,)), dma((4,)), dma((4,)), dma((4,)),
            dma((NG, 8, 4)), dma((NG, 8, 4)), dma((7,)), dma((7,)), dma((NG, 3, 4)),
            pltpu.SemaphoreType.REGULAR((NG, 4, 4)),
        ],
        compiler_params=pltpu.CompilerParams(
            collective_id=0, has_side_effects=True, vmem_limit_bytes=62 * 2**20
        ),
        cost_estimate=pl.CostEstimate(
            flops=16 * T * DB * FB, bytes_accessed=12 * DB * FB, transcendentals=T * FB
        ),
    )(layer_input, out_grad, head_depth.reshape(1, TB), gate_weight, up_weight, down_weight)


def solution(mesh):
    in_specs = (
        P("col", "row"),
        P("col", "row"),
        P("col"),
        P("row", "col"),
        P("row", "col"),
        P("col", "row"),
    )
    out_specs = (P("col", "row"), P("row", "col"), P("row", "col"), P("col", "row"))
    return jax.shard_map(body, mesh=mesh, in_specs=in_specs, out_specs=out_specs, check_vma=False)
```

time: 349 us -> 224 us (0.64)
  waiting for transfers between devices: 240 us -> 0 us
  Pallas kernels: 0 us -> 211 us
  matrix products: 43.5 us -> 0 us
  blocking collectives: 28.3 us -> 0 us
  between operations: 14.1 us -> 0.64 us
  other arithmetic: 10.9 us -> 0 us
    psum x1 -> x0, waiting for transfers between devices: 219 us -> none  [body(): lax.psum(up_part.astype(jnp.bfloat16), 'row').astype(jnp.float32)]
    pallas_call x0 -> x1, Pallas kernels: none -> 211 us  [body(): pl.pallas_call(kernel, out_shape=(jax.ShapeDtypeStruct((TB, DB), BF), jax...]
    dot_general x8 -> x0, matrix products: 43.5 us -> none  [the longest x1 10.9 us: body(): lax.dot_general(hidden, grads_all, contract_rows, preferred_element_type=...]
    all_gather x2 -> x0, blocking collectives: 28.3 us -> none  [the longest x1 14.7 us: body(): lax.all_gather(scaled, 'col', axis=0, tiled=True)]
    reduce_scatter x1 -> x0, waiting for transfers between devices: 20.6 us -> none  [body(): lax.psum_scatter(input_part.astype(jnp.bfloat16), 'col', scatter_dimensio...]
    convert_element_type x2 -> x0, other arithmetic: 10.3 us -> none  [the longest x1 9.29 us: activate(): up_act = (back_sum * silu_val).astype(jnp.bfloat16)]
    unnamed x10 -> x8, local copies, waits for them, and re-layouts: 11.8 us -> 11 us
  transfers between devices with their start and end apart: 2 -> 0, of which waited for: 2 -> 0; matrix products, arithmetic and copies ran while one was open for 3% -> 0% of each run, Pallas kernels for 0% -> 0%
where the time goes in v1:
time: 224 us; the launch traced here: 222 us
  Pallas kernels  211 us (94%)
  local copies, waits for them, and re-layouts  11 us (5%)
    pallas_call x1, Pallas kernels, body(): pl.pallas_call(kernel, out_shape=(jax.ShapeDtypeStruct((TB, DB), BF), jax...  211 us
    unnamed x8, local copies, waits for them, and re-layouts  11 us

profile of v1, /device:TPU:0, one launch (start us, length us, event | category | flops | bytes accessed | tf_op | source)
XLA Modules:
  0.0 222.5 jit_solution(6600239248260108866)
XLA Ops:
  0.6 210.8 %shard_map.93 = (bf16[96,512]{1,0:T(8,128)(2,1)}, bf16[512,3584]{1,0:T(8,128)(2,1)}, bf16[512,3584]{1,0:T(8,128)(2,1)}, bf16[3584,512]{1,0:T(8,128)(2,1)}) custom-call(bf16[96,512]{1,0:T(8,128)(2,1)} %x_ref.1, bf16[96,512]{1,0:T(8,128)(2,1)} %og_ref.1, s32[1,96]{1,0:T(1,128)} %bitcast.1, bf16[512,3584]{1,0:T(8,128)(2,1)} %wg_hbm.1, ...), custom_call_target="tpu_custom_call" | custom-call | flops 22548578304 | bytes 22020096 | tf_op jit(solution)/shard_map/pallas_call | solution.py:296
  211.5 1.5 copy.14
  213.0 0.0 copy-start.1
  213.0 4.3 %copy.15 = bf16[512,3584]{1,0:T(8,128)(2,1)} copy(bf16[512,3584]{1,0:T(8,128)(2,1)} %get-tuple-element.9) | data formatting | bytes 7340032
  217.3 0.0 copy-done.1
  217.3 0.0 copy-start
  217.3 1.9 copy.16
  219.2 1.5 copy-done
  220.7 1.8 copy.17
Async XLA Ops:
  213.0 4.3 %copy-start.1 = (bf16[512,3584]{1,0:T(8,128)(2,1)S(1)}, bf16[512,3584]{1,0:T(8,128)(2,1)}, u32[]{:S(2)}) copy-start(bf16[512,3584]{1,0:T(8,128)(2,1)} %get-tuple-element.10) | copy-start | bytes 11010052
  217.3 3.4 %copy-start = (bf16[3584,512]{1,0:T(8,128)(2,1)S(1)}, bf16[3584,512]{1,0:T(8,128)(2,1)}, u32[]{:S(2)}) copy-start(bf16[3584,512]{1,0:T(8,128)(2,1)} %get-tuple-element.11) | copy-start | bytes 11010052

commit v2 on v0

v2 whole, which is shorter than its diff:
```python
import jax
import jax.numpy as jnp
from jax import lax
from jax.experimental import pallas as pl
from jax.experimental.pallas import tpu as pltpu
from jax.sharding import PartitionSpec as P

MESH = pl.DeviceIdType.MESH
BF = jnp.bfloat16
F32 = jnp.float32

T = 768
DB = 512
FB = 3584
TB = 96
PART = FB // 4
HALF = 384
W = 128
NP = 3
ROFF = ((0, 384, 576, 672), (0, 0, 384, 576))

ORDER = (
    ("relay", 0), ("relay", 1), ("all", 3), ("relay", 2), ("relay", 3), ("near", 0), ("relay", 4), ("near", 1),
    ("near", 2), ("near", 3), ("send", 1), ("rs", 3, 0), ("rs", 0, 1), ("send", 2), ("rs", 3, 1), ("rs", 0, 2),
    ("turn", 0), ("rs", 1, 1), ("rs", 3, 2), ("rs", 0, 3), ("rs", 1, 2), ("turn", 1), ("rs", 3, 3), ("rs", 2, 1),
    ("ag", 0, 3), ("rs", 1, 3), ("turn", 2), ("rs", 2, 2), ("ag", 0, 2), ("ag", 1, 3), ("turn", 3), ("rs", 2, 3),
    ("ag", 1, 2), ("turn", 4), ("ag", 2, 3),
    ("ag", 0, 1), ("in", 0), ("theirs", 0), ("ag", 2, 2), ("ag", 1, 1), ("in", 1), ("theirs", 1),
    ("ag", 3, 3), ("own", 0), ("ag", 3, 2),
    ("ag", 2, 1), ("in", 2), ("ag", 3, 1), ("theirs", 2), ("own", 1), ("fold", 1), ("fold", 2), ("fold", 3), ("fold", 4),
    ("ag", 3, 0), ("in", 3), ("own", 2), ("fold", 0), ("own", 3),
)


def nt(a, b):
    return lax.dot_general(a, b, (((1,), (1,)), ((), ())), preferred_element_type=F32)


def nn(a, b):
    return jnp.dot(a, b, preferred_element_type=F32)


def kernel(
    x_ref, og_ref, hd_ref, wg_hbm, wu_hbm, wd_hbm,
    gi_ref, dg_hbm, du_hbm, dd_hbm,
    S, R, XS, XT, WG, WU, WD, QG, QU, QD, GI, GB, CR, HS, ZR, YS, YR,
    wsem, xs, xr, qs, qr, zs, zr, cs, cr, ss, sr, gs, gr, osem, hs, hr, free,
):
    row = lax.axis_index("row")
    col = lax.axis_index("col")
    x = lax.rem(row, 4)
    y = row // 4
    z = col // 2
    c = lax.rem(col, 2)
    rows_of = (
        y * 4 + x + 1 - 2 * lax.rem(x, 2),
        (y + 1 - 2 * lax.rem(y, 2)) * 4 + x,
        y * 4 + 3 - x,
        (3 - y) * 4 + x,
    )
    bits = (lax.rem((x + 1) // 2, 2), lax.rem((y + 1) // 2, 2), x // 2, y // 2)

    def pick(values, d):
        return jnp.where(d == 0, values[0], jnp.where(d == 1, values[1], jnp.where(d == 2, values[2], values[3])))

    def near(d):
        return (pick(rows_of, lax.rem(d, 4)), col)

    def along_z(dz):
        return (row, lax.rem(z + dz, 4) * 2 + c)

    other_core = (row, z * 2 + 1 - c)

    def first(j):
        return 0 if j == NP else 1

    def size(j, k):
        return T >> (k + 1 - first(j))

    def low(j, p, k):
        at = jnp.int32(0)
        for i in range(first(j), k):
            at = at + pick(bits, lax.rem(p + i, 4)) * size(j, i)
        return at

    def rows(at, n):
        return pl.ds(pl.multiple_of(at, 48), n)

    def held(j, p):
        return pl.ds(pl.multiple_of(p * DB + j * W, W), W)

    def place(j, p):
        if j == NP:
            at = p * PART + 2 * HALF
        else:
            at = p * PART + pick(bits, p) * HALF + j * W
        return pl.ds(pl.multiple_of(at, W), W)

    def remote(src, dst, send, recv, device):
        return pltpu.make_async_remote_copy(
            src_ref=src, dst_ref=dst, send_sem=send, recv_sem=recv, device_id=device, device_id_type=MESH
        )

    def rs_copy(j, k, p):
        n = size(j, k)
        at = low(j, p, k) + (1 - pick(bits, lax.rem(p + k, 4))) * n
        return remote(
            S.at[j, p, :, rows(at, n)], R.at[j, p, :, pl.ds(ROFF[first(j)][k], n)],
            ss.at[j, k, p], sr.at[j, k, p], near(p + k),
        )

    def ag_copy(j, k, p):
        where = S.at[j, p, :, rows(low(j, p, k + 1), size(j, k))]
        return remote(where, where, ss.at[j, 7 - k, p], sr.at[j, 7 - k, p], near(p + k))

    def load_copies(p):
        copies = []
        for i, (at, n, to) in enumerate(
            ((p * PART + pick(bits, p) * HALF, HALF, p * DB), (p * PART + 2 * HALF, W, p * DB + HALF))
        ):
            src = pl.ds(pl.multiple_of(at, W), n)
            dst = pl.ds(pl.multiple_of(to, W), n)
            copies.append(pltpu.make_async_copy(wg_hbm.at[:, src], WG.at[:, dst], wsem.at[0, p, i]))
            copies.append(pltpu.make_async_copy(wu_hbm.at[:, src], WU.at[:, dst], wsem.at[1, p, i]))
            copies.append(pltpu.make_async_copy(wd_hbm.at[src], WD.at[dst], wsem.at[2, p, i]))
        return copies

    def weight_copies(p):
        at = pl.ds(pl.multiple_of(p * PART + (1 - pick(bits, p)) * HALF, W), HALF)
        return (
            remote(wg_hbm.at[:, at], QG.at[p], qs.at[0, p], qr.at[0, p], near(p)),
            remote(wu_hbm.at[:, at], QU.at[p], qs.at[1, p], qr.at[1, p], near(p)),
            remote(wd_hbm.at[at], QD.at[p], qs.at[2, p], qr.at[2, p], near(p)),
        )

    mine = pl.ds(pl.multiple_of(col * TB, TB), TB)

    def x_copy(d):
        return remote(XS.at[0, :, mine], XS.at[1 + d, :, mine], xs.at[d], xr.at[d], near(d))

    def block(dz):
        return pl.ds(pl.multiple_of((lax.rem(z + dz + 4, 4) * 2 + c) * TB, TB), TB)

    def z_copy(b, dz):
        where = XS.at[b, :, mine]
        return remote(where, where, zs.at[b, dz], zr.at[b, dz], along_z(dz))

    def z_relay(b, dz):
        where = XS.at[b, dz // 2, block(-dz)]
        return remote(where, where, zs.at[b, dz - 1], zr.at[b, dz - 1], along_z(dz))

    def c_copy(b, dz):
        where = XS.at[b, :, block(-dz)]
        return remote(where, where, cs.at[b, dz], cr.at[b, dz], other_core)

    barrier = pltpu.get_barrier_semaphore()
    for device in [near(d) for d in range(4)] + [along_z(dz) for dz in (1, 2, 3)] + [other_core]:
        pl.semaphore_signal(barrier, inc=1, device_id=device, device_id_type=MESH)

    @pl.loop(0, 4)
    def _(p):
        for copy in load_copies(p):
            copy.start()

    depth = jnp.broadcast_to(hd_ref[...], (128, TB))
    weight = jnp.ones((128, TB), F32)
    for level in range(1, 5):
        weight = jnp.where(depth == level, F32(0.8) ** level, weight)
    weight = weight.T
    XS[0, 0, mine, :] = x_ref[...]
    for i in range(DB // 128):
        at = slice(i * 128, (i + 1) * 128)
        XS[0, 1, mine, at] = (og_ref[:, at].astype(F32) * weight).astype(BF)

    pl.semaphore_wait(barrier, 8)

    for d in range(4):
        x_copy(d).start()
    for dz in (1, 3):
        z_copy(0, dz).start()
    c_copy(0, 0).start()
    for p in range(4):
        for copy in weight_copies(p):
            copy.start()
    GI[...] = jnp.zeros_like(GI)

    @pl.loop(0, 4)
    def _(d):
        x_copy(d).wait_recv()
        for dz in (1, 3):
            z_copy(1 + d, dz).start()
        c_copy(1 + d, 0).start()

    def relay(b):
        for dz in (1, 3):
            z_copy(b, dz).wait_recv()
            z_relay(b, dz).start()
            c_copy(b, dz).start()

    def gathered(b):
        for dz in (1, 3):
            z_relay(b, dz).wait_recv()
        c_copy(b, 2).start()
        for dz in range(4):
            c_copy(b, dz).wait_recv()

    def joined(parts):
        return jnp.concatenate(parts, axis=1)

    def forward_near(p, at):
        r = rows(at, T // 2)
        cols = pl.ds(p * DB, HALF)
        gate = nn(XS[0, 0, r, :], WG[:, cols]) + nn(XS[1 + p, 0, r, :], QG[p])
        up = nn(XS[0, 0, r, :], WU[:, cols]) + nn(XS[1 + p, 0, r, :], QU[p])
        back = nt(XS[0, 1, r, :], WD[cols, :]) + nt(XS[1 + p, 1, r, :], QD[p])
        for i, part in enumerate((gate, up, back)):
            for j in range(NP):
                S[j, p, i, r, :] = part[:, j * W : (j + 1) * W].astype(BF)

    def forward_all():
        gate_w = joined([WG[:, held(NP, p)] for p in range(4)])
        up_w = joined([WU[:, held(NP, p)] for p in range(4)])
        back_w = jnp.concatenate([WD[held(NP, p), :] for p in range(4)], axis=0)
        for i in range(2):
            r = slice(i * (T // 2), (i + 1) * (T // 2))
            parts = (nn(XS[0, 0, r, :], gate_w), nn(XS[0, 0, r, :], up_w), nt(XS[0, 1, r, :], back_w))
            for m, part in enumerate(parts):
                for p in range(4):
                    S[NP, p, m, r, :] = part[:, p * W : (p + 1) * W].astype(BF)

    def send(j):
        @pl.loop(0, 4)
        def _(p):
            rs_copy(j, first(j), p).start()

    def fwd_near(p):
        gathered(1 + p)
        for copy in weight_copies(p):
            copy.wait_recv()
        bit = pick(bits, lax.rem(p + 1, 4))
        forward_near(p, (1 - bit) * (T // 2))
        rs_copy(0, 1, p).start()
        forward_near(p, bit * (T // 2))

    def rs(j, k):
        n = size(j, k)
        step = min(n, 96)

        @pl.loop(0, 4)
        def _(p):
            rs_copy(j, k, p).wait_recv()
            at = low(j, p, k + 1)
            off = ROFF[first(j)][k]
            if k < 3:
                @pl.loop(0, n // step)
                def _(i):
                    r = rows(at + i * step, step)
                    q = rows(off + i * step, step)
                    S[j, p, :, r, :] = (S[j, p, :, r, :].astype(F32) + R[j, p, :, q, :].astype(F32)).astype(BF)

                rs_copy(j, k + 1, p).start()
            else:
                r = rows(at, n)
                q = pl.ds(off, n)
                gate = S[j, p, 0, r, :].astype(F32) + R[j, p, 0, q, :].astype(F32)
                up = S[j, p, 1, r, :].astype(F32) + R[j, p, 1, q, :].astype(F32)
                back = S[j, p, 2, r, :].astype(F32) + R[j, p, 2, q, :].astype(F32)
                sig = jax.nn.sigmoid(gate)
                silu = gate * sig
                S[j, p, 0, r, :] = (silu * up).astype(BF)
                S[j, p, 1, r, :] = (back * up * (sig * (1.0 + gate * (1.0 - sig)))).astype(BF)
                S[j, p, 2, r, :] = (back * silu).astype(BF)
            rs_copy(j, k, p).wait_send()
            pl.semaphore_signal(free.at[j, k, p], inc=1, device_id=near(p + k), device_id_type=MESH)

        if k == 3:
            @pl.loop(0, 4)
            def _(p):
                gather(j, 3, p)

    def gather(j, k, p):
        pl.semaphore_wait(free.at[j, k, p], 1)
        ag_copy(j, k, p).start()

    def ag(j, k):
        @pl.loop(0, 4)
        def _(p):
            ag_copy(j, k, p).wait_recv()
            if k > first(j):
                gather(j, k - 1, p)

    def own_copies(j, p):
        src, dst = held(j, p), place(j, p)
        return (
            pltpu.make_async_copy(WG.at[:, src], dg_hbm.at[:, dst], osem.at[0, j, p]),
            pltpu.make_async_copy(WU.at[:, src], du_hbm.at[:, dst], osem.at[1, j, p]),
            pltpu.make_async_copy(WD.at[src], dd_hbm.at[dst], osem.at[2, j, p]),
        )

    def near_copies(j, p):
        src, dst = pl.ds(j * W, W), place(j, p)
        return (
            remote(QG.at[p, :, src], dg_hbm.at[:, dst], gs.at[0, j, p], gr.at[0, j, p], near(p)),
            remote(QU.at[p, :, src], du_hbm.at[:, dst], gs.at[1, j, p], gr.at[1, j, p], near(p)),
            remote(QD.at[p, src], dd_hbm.at[dst], gs.at[2, j, p], gr.at[2, j, p], near(p)),
        )

    def input_grad(j):
        at = slice(j * W, (j + 1) * W)

        def acts(p, r):
            return [S[j, p, 1, r, :], S[j, p, 2, r, :]]

        weights = []
        for p in range(4):
            weights += [WG[:, held(j, p)], WU[:, held(j, p)]]
        weights = joined(weights)
        for i in range(3):
            r = slice(i * 256, (i + 1) * 256)
            GI[0, r, :] = GI[0, r, :] + nt(joined([a for p in range(4) for a in acts(p, r)]), weights)
        if j < NP:
            @pl.loop(0, 4)
            def _(p):
                both = joined([QG[p, :, at], QU[p, :, at]])
                for i in range(3):
                    r = slice(i * 256, (i + 1) * 256)
                    GI[1 + p, r, :] = GI[1 + p, r, :] + nt(joined(acts(p, r)), both)

    def near_grads(j):
        at = slice(j * W, (j + 1) * W)

        @pl.loop(0, 4)
        def _(p):
            both = nn(XT[1 + p, 0], joined([S[j, p, 1], S[j, p, 2]])).astype(BF)
            QG[p, :, at] = both[:, :W]
            QU[p, :, at] = both[:, W:]
            QD[p, at, :] = nn(XT[1 + p, 1], S[j, p, 0]).astype(BF).T
            for copy in near_copies(j, p):
                copy.start()

    def own_grads(j):
        @pl.loop(0, 2)
        def _(i):
            for p in (2 * i, 2 * i + 1):
                both = nn(XT[0, 0], joined([S[j, p, 1], S[j, p, 2]])).astype(BF)
                WG[:, held(j, p)] = both[:, :W]
                WU[:, held(j, p)] = both[:, W:]
            down = nn(XT[0, 1], joined([S[j, 2 * i, 0], S[j, 2 * i + 1, 0]])).astype(BF)
            for n, p in enumerate((2 * i, 2 * i + 1)):
                WD[held(j, p), :] = down[:, n * W : (n + 1) * W].T
                for copy in own_copies(j, p):
                    copy.start()

    def tokens(zz, cc):
        return pl.ds(pl.multiple_of((zz * 2 + cc) * TB, TB), TB)

    def gi_core(b):
        return remote(GB.at[b], CR.at[b], hs.at[0, b], hr.at[0, b], other_core)

    def gi_z(b, dz):
        return remote(HS.at[b, dz], ZR.at[b, dz], hs.at[dz, b], hr.at[dz, b], along_z(dz))

    def gi_near(d):
        return remote(YS.at[d], YR.at[d], hs.at[4, d], hr.at[4, d], near(d))

    def gi_send(b):
        for zz in range(4):
            GB[b, zz] = GI[b, tokens(zz, 1 - c), :].astype(BF)
        gi_core(b).start()

    def gi_fold(b):
        gi_core(b).wait_recv()
        for dz in (1, 3, 2):
            zz = lax.rem(z + dz, 4)
            HS[b, dz] = (GI[b, tokens(zz, c), :] + CR[b, zz].astype(F32)).astype(BF)
            gi_z(b, dz).start()

    def gi_total(b):
        total = GI[b, mine, :] + CR[b, z].astype(F32)
        for dz in (1, 3, 2):
            gi_z(b, dz).wait_recv()
            total = total + ZR[b, dz].astype(F32)
        return total

    for what, j, *level in ORDER:
        if what == "relay":
            relay(j)
        elif what == "all":
            gathered(0)
            for p in range(4):
                for copy in load_copies(p):
                    copy.wait()
            forward_all()
            send(NP)
        elif what == "send":
            send(j)
        elif what == "near":
            fwd_near(j)
        elif what == "turn":
            XT[j, 0] = XS[j, 0].T
            XT[j, 1] = XS[j, 1].T
        elif what == "rs":
            rs(j, level[0])
        elif what == "ag":
            ag(j, level[0])
        elif what == "in":
            input_grad(j)
            if j == NP - 1:
                @pl.loop(1, 5)
                def _(b):
                    gi_send(b)
            if j == NP:
                gi_send(0)
        elif what == "fold":
            gi_fold(j)
        elif what == "theirs":
            near_grads(j)
        else:
            own_grads(j)

    @pl.loop(0, 4)
    def _(d):
        YS[d] = gi_total(1 + d).astype(BF)
        gi_near(d).start()

    total = gi_total(0)
    for d in range(4):
        gi_near(d).wait_recv()
        total = total + YR[d].astype(F32)
    gi_ref[...] = total.astype(BF)

    @pl.loop(0, 4)
    def _(p):
        x_copy(p).wait_send()
        gi_near(p).wait_send()
        for copy in weight_copies(p):
            copy.wait_send()
        for j in range(NP + 1):
            for copy in own_copies(j, p):
                copy.wait()
            for k in range(first(j), 4):
                ag_copy(j, k, p).wait_send()
            if j < NP:
                for copy in near_copies(j, p):
                    copy.wait()

    @pl.loop(0, 5)
    def _(b):
        gi_core(b).wait_send()
        for dz in range(4):
            c_copy(b, dz).wait_send()
            if dz > 0:
                gi_z(b, dz).wait_send()
        for dz in (1, 3):
            z_copy(b, dz).wait_send()
            z_relay(b, dz).wait_send()


def body(layer_input, out_grad, head_depth, gate_weight, up_weight, down_weight):
    vmem = pl.BlockSpec(memory_space=pltpu.VMEM)
    hbm = pl.BlockSpec(memory_space=pl.ANY)
    dma = pltpu.SemaphoreType.DMA
    return pl.pallas_call(
        kernel,
        out_shape=(
            jax.ShapeDtypeStruct((TB, DB), BF),
            jax.ShapeDtypeStruct((DB, FB), BF),
            jax.ShapeDtypeStruct((DB, FB), BF),
            jax.ShapeDtypeStruct((FB, DB), BF),
        ),
        in_specs=[vmem, vmem, vmem, hbm, hbm, hbm],
        out_specs=(vmem, hbm, hbm, hbm),
        scratch_shapes=[
            pltpu.VMEM((NP + 1, 4, 3, T, W), BF),
            pltpu.VMEM((NP + 1, 4, 3, 720, W), BF),
            pltpu.VMEM((5, 2, T, DB), BF),
            pltpu.VMEM((5, 2, DB, T), BF),
            pltpu.VMEM((DB, 4 * DB), BF),
            pltpu.VMEM((DB, 4 * DB), BF),
            pltpu.VMEM((4 * DB, DB), BF),
            pltpu.VMEM((4, DB, HALF), BF),
            pltpu.VMEM((4, DB, HALF), BF),
            pltpu.VMEM((4, HALF, DB), BF),
            pltpu.VMEM((5, T, DB), F32),
            pltpu.VMEM((5, 4, TB, DB), BF),
            pltpu.VMEM((5, 4, TB, DB), BF),
            pltpu.VMEM((5, 4, TB, DB), BF),
            pltpu.VMEM((5, 4, TB, DB), BF),
            pltpu.VMEM((4, TB, DB), BF),
            pltpu.VMEM((4, TB, DB), BF),
            dma((3, 4, 2)), dma((4,)), dma((4,)), dma((3, 4)), dma((3, 4)),
            dma((5, 4)), dma((5, 4)), dma((5, 4)), dma((5, 4)),
            dma((NP + 1, 8, 4)), dma((NP + 1, 8, 4)), dma((3, NP, 4)), dma((3, NP, 4)),
            dma((3, NP + 1, 4)), dma((5, 5)), dma((5, 5)),
            pltpu.SemaphoreType.REGULAR((NP + 1, 4, 4)),
        ],
        compiler_params=pltpu.CompilerParams(
            collective_id=0, has_side_effects=True, vmem_limit_bytes=63 * 2**20
        ),
        cost_estimate=pl.CostEstimate(
            flops=16 * T * DB * FB, bytes_accessed=12 * DB * FB, transcendentals=T * FB
        ),
    )(layer_input, out_grad, head_depth.reshape(1, TB), gate_weight, up_weight, down_weight)


def solution(mesh):
    in_specs = (
        P("col", "row"),
        P("col", "row"),
        P("col"),
        P("row", "col"),
        P("row", "col"),
        P("col", "row"),
    )
    out_specs = (P("col", "row"), P("row", "col"), P("row", "col"), P("col", "row"))
    return jax.shard_map(body, mesh=mesh, in_specs=in_specs, out_specs=out_specs, check_vma=False)
```

time: 349 us -> 202 us (0.58)
  waiting for transfers between devices: 240 us -> 0 us
  Pallas kernels: 0 us -> 190 us
  matrix products: 43.5 us -> 0 us
  blocking collectives: 28.3 us -> 0 us
  between operations: 14.1 us -> 0.64 us
  other arithmetic: 10.9 us -> 0 us
    psum x1 -> x0, waiting for transfers between devices: 219 us -> none  [body(): lax.psum(up_part.astype(jnp.bfloat16), 'row').astype(jnp.float32)]
    pallas_call x0 -> x1, Pallas kernels: none -> 190 us  [body(): pl.pallas_call(kernel, out_shape=(jax.ShapeDtypeStruct((TB, DB), BF), jax...]
    dot_general x8 -> x0, matrix products: 43.5 us -> none  [the longest x1 10.9 us: body(): lax.dot_general(hidden, grads_all, contract_rows, preferred_element_type=...]
    all_gather x2 -> x0, blocking collectives: 28.3 us -> none  [the longest x1 14.7 us: body(): lax.all_gather(scaled, 'col', axis=0, tiled=True)]
    reduce_scatter x1 -> x0, waiting for transfers between devices: 20.6 us -> none  [body(): lax.psum_scatter(input_part.astype(jnp.bfloat16), 'col', scatter_dimensio...]
    convert_element_type x2 -> x0, other arithmetic: 10.3 us -> none  [the longest x1 9.29 us: activate(): up_act = (back_sum * silu_val).astype(jnp.bfloat16)]
    unnamed x10 -> x8, local copies, waits for them, and re-layouts: 11.8 us -> 11 us
  transfers between devices with their start and end apart: 2 -> 0, of which waited for: 2 -> 0; matrix products, arithmetic and copies ran while one was open for 3% -> 0% of each run, Pallas kernels for 0% -> 0%
where the time goes in v2:
time: 202 us; the launch traced here: 201 us
  Pallas kernels  190 us (94%)
  local copies, waits for them, and re-layouts  11 us (5%)
    pallas_call x1, Pallas kernels, body(): pl.pallas_call(kernel, out_shape=(jax.ShapeDtypeStruct((TB, DB), BF), jax...  190 us
    unnamed x8, local copies, waits for them, and re-layouts  11 us

profile of v2, /device:TPU:0, one launch (start us, length us, event | category | flops | bytes accessed | tf_op | source)
XLA Modules:
  0.0 201.4 jit_solution(2510470053088212401)
XLA Ops:
  0.6 189.8 %shard_map.93 = (bf16[96,512]{1,0:T(8,128)(2,1)}, bf16[512,3584]{1,0:T(8,128)(2,1)}, bf16[512,3584]{1,0:T(8,128)(2,1)}, bf16[3584,512]{1,0:T(8,128)(2,1)}) custom-call(bf16[96,512]{1,0:T(8,128)(2,1)} %x_ref.1, bf16[96,512]{1,0:T(8,128)(2,1)} %og_ref.1, s32[1,96]{1,0:T(1,128)} %bitcast.1, bf16[512,3584]{1,0:T(8,128)(2,1)} %wg_hbm.1, ...), custom_call_target="tpu_custom_call" | custom-call | flops 22548578304 | bytes 22020096 | tf_op jit(solution)/shard_map/pallas_call | solution.py:463
  190.4 1.5 copy.14
  191.9 0.0 copy-start.1
  191.9 4.3 %copy.15 = bf16[512,3584]{1,0:T(8,128)(2,1)} copy(bf16[512,3584]{1,0:T(8,128)(2,1)} %get-tuple-element.9) | data formatting | bytes 7340032
  196.2 0.0 copy-done.1
  196.2 0.0 copy-start
  196.2 1.9 copy.16
  198.1 1.5 copy-done
  199.6 1.8 copy.17
Async XLA Ops:
  191.9 4.3 %copy-start.1 = (bf16[512,3584]{1,0:T(8,128)(2,1)S(1)}, bf16[512,3584]{1,0:T(8,128)(2,1)}, u32[]{:S(2)}) copy-start(bf16[512,3584]{1,0:T(8,128)(2,1)} %get-tuple-element.10) | copy-start | bytes 11010052
  196.2 3.4 %copy-start = (bf16[3584,512]{1,0:T(8,128)(2,1)S(1)}, bf16[3584,512]{1,0:T(8,128)(2,1)}, u32[]{:S(2)}) copy-start(bf16[3584,512]{1,0:T(8,128)(2,1)} %get-tuple-element.11) | copy-start | bytes 11010052

commit v3 on v2

--- a/solution.py
+++ b/solution.py
@@ -20,15 +20,17 @@
 ROFF = ((0, 384, 576, 672), (0, 0, 384, 576))
 
 ORDER = (
-    ("relay", 0), ("relay", 1), ("all", 3), ("relay", 2), ("relay", 3), ("near", 0), ("relay", 4), ("near", 1),
-    ("near", 2), ("near", 3), ("send", 1), ("rs", 3, 0), ("rs", 0, 1), ("send", 2), ("rs", 3, 1), ("rs", 0, 2),
+    ("relay", 0), ("relay", 1), ("all", 3), ("relay", 2), ("near", 0, 0), ("near", 0, 1), ("relay", 3),
+    ("near", 1, 0), ("near", 1, 1), ("relay", 4), ("near", 2, 0), ("near", 2, 1),
+    ("near", 0, 2), ("near", 1, 2), ("near", 2, 2), ("near", 3, 0), ("near", 3, 1), ("near", 3, 2), ("send", 1),
+    ("keep", 0), ("keep", 1), ("keep", 2), ("keep", 3),
+    ("rs", 3, 0), ("rs", 0, 1), ("send", 2), ("rs", 3, 1), ("rs", 0, 2),
     ("turn", 0), ("rs", 1, 1), ("rs", 3, 2), ("rs", 0, 3), ("rs", 1, 2), ("turn", 1), ("rs", 3, 3), ("rs", 2, 1),
     ("ag", 0, 3), ("rs", 1, 3), ("turn", 2), ("rs", 2, 2), ("ag", 0, 2), ("ag", 1, 3), ("turn", 3), ("rs", 2, 3),
-    ("ag", 1, 2), ("turn", 4), ("ag", 2, 3),
-    ("ag", 0, 1), ("in", 0), ("theirs", 0), ("ag", 2, 2), ("ag", 1, 1), ("in", 1), ("theirs", 1),
-    ("ag", 3, 3), ("own", 0), ("ag", 3, 2),
-    ("ag", 2, 1), ("in", 2), ("ag", 3, 1), ("theirs", 2), ("own", 1), ("fold", 1), ("fold", 2), ("fold", 3), ("fold", 4),
-    ("ag", 3, 0), ("in", 3), ("own", 2), ("fold", 0), ("own", 3),
+    ("ag", 1, 2), ("ag", 3, 3), ("turn", 4), ("ag", 2, 3),
+    ("ag", 0, 1), ("in", 0), ("theirs", 0), ("ag", 2, 2), ("ag", 3, 2), ("ag", 1, 1), ("in", 1), ("own", 0),
+    ("ag", 2, 1), ("ag", 3, 1), ("in", 2), ("theirs", 1), ("fold", 1), ("fold", 2), ("fold", 3), ("fold", 4),
+    ("theirs", 2), ("own", 1), ("ag", 3, 0), ("in", 3), ("own", 2), ("fold", 0), ("own", 3),
 )
 
 
@@ -184,18 +186,23 @@
             copy.start()
     GI[...] = jnp.zeros_like(GI)
 
-    @pl.loop(0, 4)
-    def _(d):
-        x_copy(d).wait_recv()
+    def z_send(b):
         for dz in (1, 3):
-            z_copy(1 + d, dz).start()
-        c_copy(1 + d, 0).start()
+            z_copy(b, dz).start()
 
     def relay(b):
         for dz in (1, 3):
             z_copy(b, dz).wait_recv()
             z_relay(b, dz).start()
             c_copy(b, dz).start()
+        if b == 0:
+            for d in range(4):
+                x_copy(d).wait_recv()
+                c_copy(1 + d, 0).start()
+                if d < 2:
+                    z_send(1 + d)
+        elif b < 3:
+            z_send(b + 2)
 
     def gathered(b):
         for dz in (1, 3):
@@ -207,15 +214,16 @@
     def joined(parts):
         return jnp.concatenate(parts, axis=1)
 
-    def forward_near(p, at):
+    def forward_near(p, m, at):
         r = rows(at, T // 2)
         cols = pl.ds(p * DB, HALF)
-        gate = nn(XS[0, 0, r, :], WG[:, cols]) + nn(XS[1 + p, 0, r, :], QG[p])
-        up = nn(XS[0, 0, r, :], WU[:, cols]) + nn(XS[1 + p, 0, r, :], QU[p])
-        back = nt(XS[0, 1, r, :], WD[cols, :]) + nt(XS[1 + p, 1, r, :], QD[p])
-        for i, part in enumerate((gate, up, back)):
-            for j in range(NP):
-                S[j, p, i, r, :] = part[:, j * W : (j + 1) * W].astype(BF)
+        if m < 2:
+            near_w, own_w = ((QG, WG), (QU, WU))[m]
+            part = nn(XS[0, 0, r, :], own_w[:, cols]) + nn(XS[1 + p, 0, r, :], near_w[p])
+        else:
+            part = nt(XS[0, 1, r, :], WD[cols, :]) + nt(XS[1 + p, 1, r, :], QD[p])
+        for j in range(NP):
+            S[j, p, m, r, :] = part[:, j * W : (j + 1) * W].astype(BF)
 
     def forward_all():
         gate_w = joined([WG[:, held(NP, p)] for p in range(4)])
@@ -233,14 +241,19 @@
         def _(p):
             rs_copy(j, first(j), p).start()
 
-    def fwd_near(p):
-        gathered(1 + p)
-        for copy in weight_copies(p):
-            copy.wait_recv()
+    def fwd_near(p, m):
+        if m == 0:
+            gathered(1 + p)
+        weight_copies(p)[m].wait_recv()
         bit = pick(bits, lax.rem(p + 1, 4))
-        forward_near(p, (1 - bit) * (T // 2))
-        rs_copy(0, 1, p).start()
-        forward_near(p, bit * (T // 2))
+        forward_near(p, m, (1 - bit) * (T // 2))
+        if m == 2:
+            rs_copy(0, 1, p).start()
+        else:
+            forward_near(p, m, bit * (T // 2))
+
+    def fwd_kept(p):
+        forward_near(p, 2, pick(bits, lax.rem(p + 1, 4)) * (T // 2))
 
     def rs(j, k):
         n = size(j, k)
@@ -395,7 +408,9 @@
         elif what == "send":
             send(j)
         elif what == "near":
-            fwd_near(j)
+            fwd_near(j, level[0])
+        elif what == "keep":
+            fwd_kept(j)
         elif what == "turn":
             XT[j, 0] = XS[j, 0].T
             XT[j, 1] = XS[j, 1].T
@@ -456,11 +471,29 @@
             z_relay(b, dz).wait_send()
 
 
+def copy_kernel(a, b, c, d, out_a, out_b, out_c, out_d, held_a, held_b, held_c, held_d, sem):
+    pieces = [(a, held_a, out_a)]
+    for src, mid, dst in ((b, held_b, out_b), (c, held_c, out_c), (d, held_d, out_d)):
+        n = src.shape[0] // 4
+        for k in range(4):
+            at = pl.ds(k * n, n)
+            pieces.append((src.at[at], mid.at[at], dst.at[at]))
+    reads = [pltpu.make_async_copy(src, mid, sem.at[0, i]) for i, (src, mid, dst) in enumerate(pieces)]
+    writes = [pltpu.make_async_copy(mid, dst, sem.at[1, i]) for i, (src, mid, dst) in enumerate(pieces)]
+    for read in reads:
+        read.start()
+    for read, write in zip(reads, writes):
+        read.wait()
+        write.start()
+    for write in writes:
+        write.wait()
+
+
 def body(layer_input, out_grad, head_depth, gate_weight, up_weight, down_weight):
     vmem = pl.BlockSpec(memory_space=pltpu.VMEM)
     hbm = pl.BlockSpec(memory_space=pl.ANY)
     dma = pltpu.SemaphoreType.DMA
-    return pl.pallas_call(
+    outs = pl.pallas_call(
         kernel,
         out_shape=(
             jax.ShapeDtypeStruct((TB, DB), BF),
@@ -501,6 +534,15 @@
             flops=16 * T * DB * FB, bytes_accessed=12 * DB * FB, transcendentals=T * FB
         ),
     )(layer_input, out_grad, head_depth.reshape(1, TB), gate_weight, up_weight, down_weight)
+    return pl.pallas_call(
+        copy_kernel,
+        out_shape=[jax.ShapeDtypeStruct(out.shape, out.dtype) for out in outs],
+        in_specs=[hbm] * 4,
+        out_specs=[hbm] * 4,
+        scratch_shapes=[pltpu.VMEM(out.shape, out.dtype) for out in outs] + [dma((2, 13))],
+        compiler_params=pltpu.CompilerParams(vmem_limit_bytes=63 * 2**20),
+        cost_estimate=pl.CostEstimate(flops=0, bytes_accessed=12 * DB * FB, transcendentals=0),
+    )(*outs)
 
 
 def solution(mesh):

time: 202 us -> 184 us (0.911)
  local copies, waits for them, and re-layouts: 11 us -> 0 us
  Pallas kernels: 190 us -> 183 us
    pallas_call x1, Pallas kernels: 190 us -> 174 us  [body(): pl.pallas_call(kernel, out_shape=(jax.ShapeDtypeStruct((TB, DB), BF), jax...]
    unnamed x8 -> x0, local copies, waits for them, and re-layouts: 11 us -> none
    pallas_call x0 -> x1, Pallas kernels: none -> 8.69 us  [body(): pl.pallas_call(copy_kernel, out_shape=[jax.ShapeDtypeStruct(out.shape, ou...]
where the time goes in v3:
time: 184 us
  Pallas kernels  183 us (99%)
    pallas_call x1, Pallas kernels, body(): pl.pallas_call(kernel, out_shape=(jax.ShapeDtypeStruct((TB, DB), BF), jax...  174 us
    pallas_call x1, Pallas kernels, body(): pl.pallas_call(copy_kernel, out_shape=[jax.ShapeDtypeStruct(out.shape, ou...  8.69 us

profile of v3, /device:TPU:0, one launch (start us, length us, event | category | flops | bytes accessed | tf_op | source)
XLA Modules:
  0.0 183.5 jit_solution(18212549757922212769)
XLA Ops:
  0.6 174.0 %shard_map.93 = (bf16[96,512]{1,0:T(8,128)(2,1)}, bf16[512,3584]{1,0:T(8,128)(2,1)}, bf16[512,3584]{1,0:T(8,128)(2,1)}, bf16[3584,512]{1,0:T(8,128)(2,1)}) custom-call(bf16[96,512]{1,0:T(8,128)(2,1)} %x_ref.1, bf16[96,512]{1,0:T(8,128)(2,1)} %og_ref.1, s32[1,96]{1,0:T(1,128)} %bitcast.1, bf16[512,3584]{1,0:T(8,128)(2,1)} %wg_hbm.1, ...), custom_call_target="tpu_custom_call" | custom-call | flops 22548578304 | bytes 22020096 | tf_op jit(solution)/shard_map/pallas_call | solution.py:496
  174.7 8.7 %shard_map.94 = (bf16[96,512]{1,0:T(8,128)(2,1)}, bf16[512,3584]{1,0:T(8,128)(2,1)}, bf16[512,3584]{1,0:T(8,128)(2,1)}, bf16[3584,512]{1,0:T(8,128)(2,1)}) custom-call(bf16[96,512]{1,0:T(8,128)(2,1)} %get-tuple-element.8.a, bf16[512,3584]{1,0:T(8,128)(2,1)} %get-tuple-element.9.b, bf16[512,3584]{1,0:T(8,128)(2,1)} %get-tuple-element.10.c, ...), custom_call_target="tpu_custom_call" | custom-call | bytes 22020096 | tf_op jit(solution)/shard_map/pallas_call | solution.py:537

commit v4 on v3

--- a/solution.py
+++ b/solution.py
@@ -28,9 +28,9 @@
     ("turn", 0), ("rs", 1, 1), ("rs", 3, 2), ("rs", 0, 3), ("rs", 1, 2), ("turn", 1), ("rs", 3, 3), ("rs", 2, 1),
     ("ag", 0, 3), ("rs", 1, 3), ("turn", 2), ("rs", 2, 2), ("ag", 0, 2), ("ag", 1, 3), ("turn", 3), ("rs", 2, 3),
     ("ag", 1, 2), ("ag", 3, 3), ("turn", 4), ("ag", 2, 3),
-    ("ag", 0, 1), ("in", 0), ("theirs", 0), ("ag", 2, 2), ("ag", 3, 2), ("ag", 1, 1), ("in", 1), ("own", 0),
-    ("ag", 2, 1), ("ag", 3, 1), ("in", 2), ("theirs", 1), ("fold", 1), ("fold", 2), ("fold", 3), ("fold", 4),
-    ("theirs", 2), ("own", 1), ("ag", 3, 0), ("in", 3), ("own", 2), ("fold", 0), ("own", 3),
+    ("ag", 0, 1), ("in", 0), ("ag", 2, 2), ("theirs", 0), ("ag", 3, 2), ("ag", 1, 1), ("in", 1),
+    ("ag", 2, 1), ("ag", 3, 1), ("in", 2), ("fold", 1), ("fold", 2), ("fold", 3), ("fold", 4), ("theirs", 1),
+    ("theirs", 2), ("own", 0), ("ag", 3, 0), ("in", 3), ("own", 1), ("fold", 0), ("own", 2), ("own", 3),
 )
 
 
@@ -324,6 +324,16 @@
         def acts(p, r):
             return [S[j, p, 1, r, :], S[j, p, 2, r, :]]
 
+        if j < NP:
+            @pl.loop(0, 4)
+            def _(p):
+                both = joined([QG[p, :, at], QU[p, :, at]])
+                for i in range(3):
+                    r = slice(i * 256, (i + 1) * 256)
+                    GI[1 + p, r, :] = GI[1 + p, r, :] + nt(joined(acts(p, r)), both)
+                if j == NP - 1:
+                    gi_send(1 + p)
+
         weights = []
         for p in range(4):
             weights += [WG[:, held(j, p)], WU[:, held(j, p)]]
@@ -331,13 +341,8 @@
         for i in range(3):
             r = slice(i * 256, (i + 1) * 256)
             GI[0, r, :] = GI[0, r, :] + nt(joined([a for p in range(4) for a in acts(p, r)]), weights)
-        if j < NP:
-            @pl.loop(0, 4)
-            def _(p):
-                both = joined([QG[p, :, at], QU[p, :, at]])
-                for i in range(3):
-                    r = slice(i * 256, (i + 1) * 256)
-                    GI[1 + p, r, :] = GI[1 + p, r, :] + nt(joined(acts(p, r)), both)
+        if j == NP:
+            gi_send(0)
 
     def near_grads(j):
         at = slice(j * W, (j + 1) * W)
@@ -420,12 +425,6 @@
             ag(j, level[0])
         elif what == "in":
             input_grad(j)
-            if j == NP - 1:
-                @pl.loop(1, 5)
-                def _(b):
-                    gi_send(b)
-            if j == NP:
-                gi_send(0)
         elif what == "fold":
             gi_fold(j)
         elif what == "theirs":

time: 184 us -> 183 us (level)
  Pallas kernels: 183 us -> 181 us
    pallas_call x1, Pallas kernels: 174 us -> 172 us  [body(): pl.pallas_call(kernel, out_shape=(jax.ShapeDtypeStruct((TB, DB), BF), jax...]
where the time goes in v4:
time: 183 us; the launch traced here: 182 us
  Pallas kernels  181 us (99%)
    pallas_call x1, Pallas kernels, body(): pl.pallas_call(kernel, out_shape=(jax.ShapeDtypeStruct((TB, DB), BF), jax...  172 us
    pallas_call x1, Pallas kernels, body(): pl.pallas_call(copy_kernel, out_shape=[jax.ShapeDtypeStruct(out.shape, ou...  8.69 us

profile of v4, /device:TPU:0, one launch (start us, length us, event | category | flops | bytes accessed | tf_op | source)
XLA Modules:
  0.0 181.6 jit_solution(11307212990602353120)
XLA Ops:
  0.6 172.1 %shard_map.93 = (bf16[96,512]{1,0:T(8,128)(2,1)}, bf16[512,3584]{1,0:T(8,128)(2,1)}, bf16[512,3584]{1,0:T(8,128)(2,1)}, bf16[3584,512]{1,0:T(8,128)(2,1)}) custom-call(bf16[96,512]{1,0:T(8,128)(2,1)} %x_ref.1, bf16[96,512]{1,0:T(8,128)(2,1)} %og_ref.1, s32[1,96]{1,0:T(1,128)} %bitcast.1, bf16[512,3584]{1,0:T(8,128)(2,1)} %wg_hbm.1, ...), custom_call_target="tpu_custom_call" | custom-call | flops 22548578304 | bytes 22020096 | tf_op jit(solution)/shard_map/pallas_call | solution.py:495
  172.7 8.7 %shard_map.94 = (bf16[96,512]{1,0:T(8,128)(2,1)}, bf16[512,3584]{1,0:T(8,128)(2,1)}, bf16[512,3584]{1,0:T(8,128)(2,1)}, bf16[3584,512]{1,0:T(8,128)(2,1)}) custom-call(bf16[96,512]{1,0:T(8,128)(2,1)} %get-tuple-element.8.a, bf16[512,3584]{1,0:T(8,128)(2,1)} %get-tuple-element.9.b, bf16[512,3584]{1,0:T(8,128)(2,1)} %get-tuple-element.10.c, ...), custom_call_target="tpu_custom_call" | custom-call | bytes 22020096 | tf_op jit(solution)/shard_map/pallas_call | solution.py:536

commit v5 on v4

--- a/solution.py
+++ b/solution.py
@@ -20,13 +20,13 @@
 ROFF = ((0, 384, 576, 672), (0, 0, 384, 576))
 
 ORDER = (
-    ("relay", 0), ("relay", 1), ("all", 3), ("relay", 2), ("near", 0, 0), ("near", 0, 1), ("relay", 3),
-    ("near", 1, 0), ("near", 1, 1), ("relay", 4), ("near", 2, 0), ("near", 2, 1),
+    ("relay", 0), ("relay", 1), ("all", 3), ("turn", 0), ("relay", 2), ("near", 0, 0), ("near", 0, 1), ("turn", 1), ("relay", 3),
+    ("near", 1, 0), ("near", 1, 1), ("turn", 2), ("relay", 4), ("near", 2, 0), ("near", 2, 1),
     ("near", 0, 2), ("near", 1, 2), ("near", 2, 2), ("near", 3, 0), ("near", 3, 1), ("near", 3, 2), ("send", 1),
     ("keep", 0), ("keep", 1), ("keep", 2), ("keep", 3),
     ("rs", 3, 0), ("rs", 0, 1), ("send", 2), ("rs", 3, 1), ("rs", 0, 2),
-    ("turn", 0), ("rs", 1, 1), ("rs", 3, 2), ("rs", 0, 3), ("rs", 1, 2), ("turn", 1), ("rs", 3, 3), ("rs", 2, 1),
-    ("ag", 0, 3), ("rs", 1, 3), ("turn", 2), ("rs", 2, 2), ("ag", 0, 2), ("ag", 1, 3), ("turn", 3), ("rs", 2, 3),
+    ("rs", 1, 1), ("rs", 3, 2), ("rs", 0, 3), ("rs", 1, 2), ("rs", 3, 3), ("rs", 2, 1),
+    ("ag", 0, 3), ("rs", 1, 3), ("rs", 2, 2), ("ag", 0, 2), ("ag", 1, 3), ("turn", 3), ("rs", 2, 3),
     ("ag", 1, 2), ("ag", 3, 3), ("turn", 4), ("ag", 2, 3),
     ("ag", 0, 1), ("in", 0), ("ag", 2, 2), ("theirs", 0), ("ag", 3, 2), ("ag", 1, 1), ("in", 1),
     ("ag", 2, 1), ("ag", 3, 1), ("in", 2), ("fold", 1), ("fold", 2), ("fold", 3), ("fold", 4), ("theirs", 1),

time: 183 us -> 183 us (level)
  no operation moved by 1% of the time
where the time goes in v5:
time: 183 us; the launch traced here: 182 us
  Pallas kernels  181 us (99%)
    pallas_call x1, Pallas kernels, body(): pl.pallas_call(kernel, out_shape=(jax.ShapeDtypeStruct((TB, DB), BF), jax...  172 us
    pallas_call x1, Pallas kernels, body(): pl.pallas_call(copy_kernel, out_shape=[jax.ShapeDtypeStruct(out.shape, ou...  8.69 us

profile of v5, /device:TPU:0, one launch (start us, length us, event | category | flops | bytes accessed | tf_op | source)
XLA Modules:
  0.0 181.6 jit_solution(11471421391898484691)
XLA Ops:
  0.6 172.1 %shard_map.93 = (bf16[96,512]{1,0:T(8,128)(2,1)}, bf16[512,3584]{1,0:T(8,128)(2,1)}, bf16[512,3584]{1,0:T(8,128)(2,1)}, bf16[3584,512]{1,0:T(8,128)(2,1)}) custom-call(bf16[96,512]{1,0:T(8,128)(2,1)} %x_ref.1, bf16[96,512]{1,0:T(8,128)(2,1)} %og_ref.1, s32[1,96]{1,0:T(1,128)} %bitcast.1, bf16[512,3584]{1,0:T(8,128)(2,1)} %wg_hbm.1, ...), custom_call_target="tpu_custom_call" | custom-call | flops 22548578304 | bytes 22020096 | tf_op jit(solution)/shard_map/pallas_call | solution.py:495
  172.7 8.7 %shard_map.94 = (bf16[96,512]{1,0:T(8,128)(2,1)}, bf16[512,3584]{1,0:T(8,128)(2,1)}, bf16[512,3584]{1,0:T(8,128)(2,1)}, bf16[3584,512]{1,0:T(8,128)(2,1)}) custom-call(bf16[96,512]{1,0:T(8,128)(2,1)} %get-tuple-element.8.a, bf16[512,3584]{1,0:T(8,128)(2,1)} %get-tuple-element.9.b, bf16[512,3584]{1,0:T(8,128)(2,1)} %get-tuple-element.10.c, ...), custom_call_target="tpu_custom_call" | custom-call | bytes 22020096 | tf_op jit(solution)/shard_map/pallas_call | solution.py:536
